TPU v7x, 32 devices: a whole 2x2x4 slice. The times are simulated.
32 devices in a mesh: row: 8 (over z, core), col: 4 (over y, x).
Axes of the slice: x: 2, y: 2, z: 4, core: 2. Of those that a mesh axis runs over, the one named last changes fastest.
Arguments:
- trailing: float32 [4096, 4096], P('row', 'col'), may hold values from -6 to 6
- panel: float32 [4096, 512], P(('row', 'col')), may hold values from -0.25 to 0.25
- inv_factor: float32 [512, 512], P(None, 'col'), as said below
- later_series: float32 [4096, 1024], P('row', 'col'), may hold values from -6 to 6
- fold_series: float32 [512, 1024], P('row', 'col'), may hold values from -6 to 6
- fold_len: int32 [1024], P('col'), may hold values from 1 to 8, as said below
Outputs:
- new_trailing: float32 [4096, 4096], P('row', 'col')
- new_series: float32 [4096, 1024], P('row', 'col')
Inputs may be any that keep to these rules, and one draw needn't show every extreme that they name: inv_factor is lower triangular with a diagonal between 1 and 2. `fold_len`: some series reach all 8 blocks and some only one.
All inputs are finite; a program needn't handle non-finite values.
Results may differ from a plain program's by a relative error of at most 0.0003.
Values sent between devices are 32-bit elements; how exact they have to be, the bound alone decides.
A program may use at most 64 MiB of HBM per device.

v0:
```python
import jax
import jax.numpy as jnp
from jax import lax
from jax.sharding import PartitionSpec as P


def on_device(trailing, panel, inv_factor, later_series, fold_series, fold_len):
    highest = lax.Precision.HIGHEST
    contract = (((1,), (1,)), ((), ()))
    inverse = lax.all_gather(inv_factor, "col", axis=1, tiled=True)
    solved_mine = lax.dot_general(
        panel, inverse, contract, precision=highest, preferred_element_type=jnp.float32
    )
    row_block = lax.all_gather(solved_mine, "col", axis=0, tiled=True)
    rows_here = trailing.shape[0]
    cols_here = trailing.shape[1]
    tiles_across = cols_here // rows_here
    row_pos = lax.axis_index("row")
    col_pos = lax.axis_index("col")
    piece_rows = solved_mine.shape[0]
    width = solved_mine.shape[1]
    groups = lax.axis_size("col")
    gathered = lax.all_gather(solved_mine, "row", axis=0, tiled=True)
    grouped = gathered.reshape(groups, tiles_across, piece_rows, width)
    swapped = lax.all_to_all(grouped, "col", split_axis=0, concat_axis=0, tiled=True)
    col_panel = jnp.transpose(swapped, (1, 0, 2, 3)).reshape(
        tiles_across * groups * piece_rows, width
    )
    update = lax.dot_general(
        row_block, col_panel, contract, precision=highest, preferred_element_type=jnp.float32
    )
    col_tile = (col_pos * cols_here + jnp.arange(cols_here, dtype=jnp.int32)) // rows_here
    lower = col_tile <= row_pos
    new_trailing = jnp.where(lower[None, :], trailing - update, trailing)
    fold_all = lax.all_gather(fold_series, "row", axis=0, tiled=True)
    innovations = jnp.dot(inverse, fold_all, precision=highest, preferred_element_type=jnp.float32)
    correction = jnp.dot(
        row_block, innovations, precision=highest, preferred_element_type=jnp.float32
    )
    active = row_pos < fold_len
    new_series = jnp.where(active[None, :], later_series - correction, later_series)
    return (new_trailing, new_series)


def solution(mesh):
    in_specs = (
        P("row", "col"),
        P(("row", "col"), None),
        P(None, "col"),
        P("row", "col"),
        P("row", "col"),
        P("col"),
    )
    out_specs = (P("row", "col"), P("row", "col"))
    return jax.shard_map(
        on_device, mesh=mesh, in_specs=in_specs, out_specs=out_specs, check_vma=False
    )
```

profile of v0, /device:TPU:0, one launch (start us, length us, event | category | flops | bytes accessed | tf_op | source)
XLA Modules:
  0.0 126.2 jit_solution(1465415909796620497)
XLA Ops:
  7.2 0.0 copy-start
  7.2 0.0 all-gather.4.cloned.1.call-start
  7.2 0.7 all-gather.4.cloned.1.call-update
  7.9 0.0 all-gather.8.cloned.1.call-start
  8.0 31.1 %all-gather.4.cloned.1.call-done = f32[512,512]{1,0:T(8,128)} async-done(((f32[512,128]{1,0:T(8,128)}), f32[512,512]{1,0:T(8,128)}) %all-gather.4.cloned.1.call-update) | async-done | bytes 1048592 | tf_op jit(solution)/shard_map/all_gather | solution.py:10
  39.1 0.0 copy-done
  39.1 3.1 %fusion.5 = f32[128,512]{1,0:T(8,128)} fusion(f32[128,512]{1,0:T(8,128)S(1)} %copy-done, f32[512,512]{1,0:T(8,128)} %all-gather.4.cloned.1.call-done), kind=kOutput, calls=%fused_computation.14 | convolution fusion | flops 402653184 | bytes 1572864 | tf_op jit(solution)/shard_map/dot_general | solution.py:11
  42.2 0.0 all-gather.8.cloned.1.call-update
  42.2 0.0 all-gather.6.cloned.1.call-start
  42.2 0.7 all-gather.6.cloned.1.call-update
  42.9 28.5 %all-gather.8.cloned.1.call-done = f32[1024,512]{1,0:T(8,128)} async-done(((f32[128,512]{1,0:T(8,128)}), f32[1024,512]{1,0:T(8,128)}) %all-gather.8.cloned.1.call-update) | async-done | bytes 2097168 | tf_op jit(solution)/shard_map/all_gather | solution.py:23
  71.4 0.0 copy-start.5
  71.4 0.0 copy-start.4
  71.4 0.0 copy-start.1
  71.4 3.8 %all-to-all-start = ((f32[4,2,128,512]{3,2,1,0:T(8,128)}), f32[4,2,128,512]{3,2,1,0:T(8,128)S(1)}, u32[]{:S(2)}, u32[]{:S(2)}) async-start(f32[4,2,128,512]{3,2,1,0:T(8,128)} %bitcast.13), calls=%async_computation | async-start | bytes 4194304 | tf_op jit(solution)/shard_map/all_to_all | solution.py:25
  75.2 0.0 copy-done.5
  75.3 0.0 copy-done.4
  75.3 14.6 %all_gather.15 = f32[512,256]{1,0:T(8,128)S(1)} all-gather(f32[64,256]{1,0:T(8,128)S(1)} %copy-done.4), channel_id=1, replica_groups=mesh['row'=8,'col'=4] {'row'}, dimensions={0}, use_global_device_ids=true | all-gather | bytes 589824 | tf_op jit(solution)/shard_map/all_gather | solution.py:35
  89.9 0.0 copy-done.1
  89.9 1.8 %fusion.6 = f32[512,256]{1,0:T(8,128)} fusion(f32[512,512]{1,0:T(8,128)S(1)} %copy-done.1, f32[512,256]{1,0:T(8,128)S(1)} %all_gather.15), kind=kOutput, calls=%fused_computation.15 | convolution fusion | flops 805306368 | bytes 2097152 | tf_op jit(solution)/shard_map/dot_general | solution.py:36
  91.7 17.8 %all-gather.6.cloned.1.call-done = f32[512,512]{1,0:T(8,128)} async-done(((f32[128,512]{1,0:T(8,128)}), f32[512,512]{1,0:T(8,128)}) %all-gather.6.cloned.1.call-update) | async-done | bytes 1048592 | tf_op jit(solution)/shard_map/all_gather | solution.py:14
  109.5 3.3 %fusion = f32[512,256]{1,0:T(8,128)} fusion(f32[512,256]{1,0:T(8,128)} %param.9, f32[512,512]{1,0:T(8,128)} %all-gather.6.cloned.1.call-done, f32[512,256]{1,0:T(8,128)} %fusion.6, pred[256]{0:T(512)(128)(4,1)S(1)} %broadcast_compare_fusion), kind=kOutput, calls=%fused_computation.2 | convolution fusion | flops 805568512 | bytes 2621696 | tf_op jit(solution)/shard_map/dot_general | solution.py:37
  112.8 0.0 copy-start.2
  112.8 0.0 all-to-all-done
  112.8 0.0 copy-start.3
  112.8 0.2 copy.9
  113.0 1.0 copy-done.2
  114.0 0.7 copy-done.3
  114.7 5.0 %subtract_select_fusion = f32[512,1024]{1,0:T(8,128)} fusion(f32[512,1024]{1,0:T(8,128)S(1)} %copy-done.3, f32[512,512]{1,0:T(8,128)S(1)} %copy-done.2, f32[1024,512]{1,0:T(8,128)S(1)} %bitcast.12, pred[1024]{0:T(1024)(128)(4,1)S(1)} %fusion.2), kind=kOutput, calls=%fused_computation | convolution fusion | flops 3222274048 | bytes 7341056 | tf_op jit(solution)/shard_map/dot_general | solution.py:29
  (2 shorter events, 0.0 us)
Async XLA Ops:
  7.2 31.9 %copy-start = (f32[128,512]{1,0:T(8,128)S(1)}, f32[128,512]{1,0:T(8,128)}, u32[]{:S(2)}) copy-start(f32[128,512]{1,0:T(8,128)} %param.7) | copy-start | bytes 786436
  7.2 31.9 %all-gather.4.cloned.1.call-start = ((), (), s32[]{:S(2)}) async-start(), calls=%async_computation.1 | async-start | bytes 1310720 | tf_op jit(solution)/shard_map/all_gather | solution.py:10
  7.9 63.5 %all-gather.8.cloned.1.call-start = ((), (), s32[]{:S(2)}) async-start(), calls=%async_computation.3 | async-start | bytes 2359296 | tf_op jit(solution)/shard_map/all_gather | solution.py:23
  42.2 67.3 %all-gather.6.cloned.1.call-start = ((), (), s32[]{:S(2)}) async-start(), calls=%async_computation.2 | async-start | bytes 1310720 | tf_op jit(solution)/shard_map/all_gather | solution.py:14
  71.4 3.8 %copy-start.5 = (s32[256]{0:T(256)S(1)}, s32[256]{0:T(256)}, u32[]{:S(2)}) copy-start(s32[256]{0:T(256)} %param.11) | copy-start | bytes 3076
  71.4 3.8 %copy-start.4 = (f32[64,256]{1,0:T(8,128)S(1)}, f32[64,256]{1,0:T(8,128)}, u32[]{:S(2)}) copy-start(f32[64,256]{1,0:T(8,128)} %param.10) | copy-start | bytes 196612
  71.4 18.5 %copy-start.1 = (f32[512,512]{1,0:T(8,128)S(1)}, f32[512,512]{1,0:T(8,128)}, u32[]{:S(2)}) copy-start(f32[512,512]{1,0:T(8,128)} %all-gather.4.cloned.1.call-done) | copy-start | bytes 3145732
  71.4 41.3 %all-to-all-start = ((f32[4,2,128,512]{3,2,1,0:T(8,128)}), f32[4,2,128,512]{3,2,1,0:T(8,128)S(1)}, u32[]{:S(2)}, u32[]{:S(2)}) async-start(f32[4,2,128,512]{3,2,1,0:T(8,128)} %bitcast.13), calls=%async_computation | async-start | bytes 4194304 | tf_op jit(solution)/shard_map/all_to_all | solution.py:25
  112.8 1.2 copy-start.2
  112.8 1.9 %copy-start.3 = (f32[512,1024]{1,0:T(8,128)S(1)}, f32[512,1024]{1,0:T(8,128)}, u32[]{:S(2)}) copy-start(f32[512,1024]{1,0:T(8,128)} %param.6) | copy-start | bytes 6291460
Sparse Core Ops, SparseCore 0:
  9.8 29.1 all-gather.3
  42.3 29.0 all-gather.7
  73.9 35.5 all-gather.5
where the time goes:
time: 127 us; the launch traced here: 126 us
  waiting for transfers between devices  78.8 us (62%)
  blocking collectives  14.6 us (11%)
  between operations  13.8 us (11%)
  matrix products  13.2 us (10%)
  starting transfers between devices  3.9 us (3%)
  local copies, waits for them, and re-layouts  1.93 us (2%)
    all_gather x1, waiting for transfers between devices, on_device(): inverse = lax.all_gather(inv_factor, 'col', axis=1, tiled=True)  31.1 us
    all_gather x1, waiting for transfers between devices, on_device(): gathered = lax.all_gather(solved_mine, 'row', axis=0, tiled=True)  28.5 us
    all_gather x1, waiting for transfers between devices, on_device(): row_block = lax.all_gather(solved_mine, 'col', axis=0, tiled=True)  17.8 us
    all_gather x1, blocking collectives, on_device(): fold_all = lax.all_gather(fold_series, 'row', axis=0, tiled=True)  14.6 us
    dot_general x1, matrix products, on_device(): lax.dot_general(row_block, col_panel, contract, precision=highest, prefer...  5 us
    all_to_all x1, starting transfers between devices, on_device(): lax.all_to_all(grouped, 'col', split_axis=0, concat_axis=0, tiled=True)  3.78 us
    dot_general x1, matrix products, on_device(): jnp.dot(row_block, innovations, precision=highest, preferred_element_type...  3.3 us
    dot_general x1, matrix products, on_device(): lax.dot_general(panel, inverse, contract, precision=highest, preferred_el...  3.09 us
  transfers between devices with their start and end apart: 4, of which 3 were waited for; matrix products, arithmetic and copies ran while one was open for 4% of the time, Pallas kernels for 0%

commit v1 on v0

v1 whole, which is shorter than its diff:
```python
import functools

import jax
import jax.numpy as jnp
from jax import lax
from jax.experimental import pallas as pl
from jax.experimental.pallas import tpu as pltpu
from jax.sharding import PartitionSpec as P

MESH = pl.DeviceIdType.MESH
F32 = jnp.float32
BF16 = jnp.bfloat16
NT = (((1,), (1,)), ((), ()))
NN = (((1,), (0,)), ((), ()))


def split(x):
    high = x.astype(BF16)
    return high, (x - high.astype(F32)).astype(BF16)


def dot3(a, b, dims):
    dot = functools.partial(lax.dot_general, dimension_numbers=dims, preferred_element_type=F32)
    return dot(a[0], b[0]) + (dot(a[0], b[1]) + dot(a[1], b[0]))


def kernel(
    planes, groups, chunks,
    panel_ref, inv_ref, fold_ref,
    update_ref, corr_ref,
    tiles, inv_t, fold, q_hi, q_lo, g_hi, g_lo,
    rb_send, rb_recv, up_send, up_recv, sib_send, sib_recv,
    fold_send, fold_recv, fsib_send, fsib_recv,
    inv_send, inv_recv, isib_send, isib_recv,
):
    row = lax.axis_index("row")
    c = lax.axis_index("col")
    z = row // 2
    k = row % 2
    piece = panel_ref.shape[0]
    step = piece // chunks
    width = panel_ref.shape[1]
    fold_rows = fold_ref.shape[0]
    inv_cols = inv_ref.shape[1]
    half = inv_cols // 2
    sibling = (2 * z + (1 - k), c)

    barrier = pltpu.get_barrier_semaphore()
    pl.semaphore_signal(barrier, inc=1, device_id=sibling, device_id_type=MESH)
    for o in range(1, planes):
        pl.semaphore_signal(
            barrier, inc=1, device_id=(2 * ((z + o) % planes) + k, c), device_id_type=MESH
        )
    for o in range(1, groups):
        pl.semaphore_signal(
            barrier, inc=1, device_id=(row, (c + o) % groups), device_id_type=MESH
        )

    def slot_of(col):
        return jnp.where(col == z, k, 2)

    slot = slot_of(c)

    def rows_of(j, h):
        return pl.ds(pl.multiple_of(j * piece + h * step, step), step)

    def rb_copy(o, h):
        target = (c + o) % groups
        return pltpu.make_async_remote_copy(
            src_ref=tiles.at[slot, rows_of(c, h)],
            dst_ref=tiles.at[slot_of(target), rows_of(c, h)],
            send_sem=rb_send.at[o, h],
            recv_sem=rb_recv.at[c, h],
            device_id=(row, target),
            device_id_type=MESH,
        )

    def rb_arrival(j, h):
        return pltpu.make_async_remote_copy(
            src_ref=tiles.at[slot, rows_of(j, h)],
            dst_ref=tiles.at[slot, rows_of(j, h)],
            send_sem=rb_send.at[0, h],
            recv_sem=rb_recv.at[j, h],
            device_id=sibling,
            device_id_type=MESH,
        )

    def up_copy(j, h):
        return pltpu.make_async_remote_copy(
            src_ref=tiles.at[k, rows_of(j, h)],
            dst_ref=tiles.at[k, rows_of(j, h)],
            send_sem=up_send.at[j, h],
            recv_sem=up_recv.at[j, h],
            device_id=(jnp.minimum(row + 2, 2 * planes - 2 + k), c),
            device_id_type=MESH,
        )

    def sib_copy(tile, j, h):
        return pltpu.make_async_remote_copy(
            src_ref=tiles.at[tile, rows_of(j, h)],
            dst_ref=tiles.at[tile, rows_of(j, h)],
            send_sem=sib_send.at[j, h],
            recv_sem=sib_recv.at[j, h],
            device_id=sibling,
            device_id_type=MESH,
        )

    def fold_at(plane, core):
        return fold.at[pl.ds(pl.multiple_of((2 * plane + core) * fold_rows, fold_rows), fold_rows)]

    def fold_copy(o):
        target = (z + o) % planes
        return pltpu.make_async_remote_copy(
            src_ref=fold_at(z, k),
            dst_ref=fold_at(z, k),
            send_sem=fold_send.at[o],
            recv_sem=fold_recv.at[planes - o],
            device_id=(2 * target + k, c),
            device_id_type=MESH,
        )

    def fold_arrival(o):
        ref = fold_at((z + o) % planes, k)
        return pltpu.make_async_remote_copy(
            src_ref=ref, dst_ref=ref, send_sem=fold_send.at[0], recv_sem=fold_recv.at[o],
            device_id=sibling, device_id_type=MESH,
        )

    def fsib_copy(o, core):
        ref = fold_at((z + o) % planes, core)
        return pltpu.make_async_remote_copy(
            src_ref=ref, dst_ref=ref, send_sem=fsib_send.at[o], recv_sem=fsib_recv.at[o],
            device_id=sibling, device_id_type=MESH,
        )

    def inv_at(col, core):
        return inv_t.at[pl.ds(pl.multiple_of(col * inv_cols + core * half, half), half)]

    def inv_copy(o):
        return pltpu.make_async_remote_copy(
            src_ref=inv_at(c, k),
            dst_ref=inv_at(c, k),
            send_sem=inv_send.at[o],
            recv_sem=inv_recv.at[groups - o],
            device_id=(row, (c + o) % groups),
            device_id_type=MESH,
        )

    def inv_arrival(o):
        ref = inv_at((c + o) % groups, k)
        return pltpu.make_async_remote_copy(
            src_ref=ref, dst_ref=ref, send_sem=inv_send.at[0], recv_sem=inv_recv.at[o],
            device_id=sibling, device_id_type=MESH,
        )

    def isib_copy(o, core):
        ref = inv_at((c + o) % groups, core)
        return pltpu.make_async_remote_copy(
            src_ref=ref, dst_ref=ref, send_sem=isib_send.at[o], recv_sem=isib_recv.at[o],
            device_id=sibling, device_id_type=MESH,
        )

    has_tiles = z >= c
    relays = has_tiles & (z + 1 < planes)
    gives = (z > c) | ((z == c) & (k == 0))
    takes = (z > c) | ((z == c) & (k == 1))

    own = pl.ds(pl.multiple_of(c * piece, piece), piece)
    tiles[slot, own, :] = panel_ref[...]
    fold[pl.ds(pl.multiple_of(row * fold_rows, fold_rows), fold_rows), :] = fold_ref[...]
    inv_t[pl.ds(pl.multiple_of(c * inv_cols, inv_cols), inv_cols), :] = inv_ref[...].T

    pl.semaphore_wait(barrier, planes + groups - 1)

    def chain(j):
        for h in range(chunks):
            @pl.when(z > c)
            def _():
                up_copy(j, h).wait_recv()

            @pl.when((z == c) & (c != j))
            def _():
                rb_arrival(j, h).wait_recv()

            @pl.when(relays)
            def _():
                up_copy(j, h).start()

            @pl.when(gives)
            def _():
                sib_copy(k, j, h).start()

    for h in range(chunks):
        for o in range(1, groups):
            rb_copy(o, h).start()
    fsib_copy(0, k).start()
    for o in range(1, planes):
        fold_copy(o).start()
    for o in range(1, groups):
        inv_copy(o).start()

    per = max(1, min(groups, 256 // piece))
    halfway = groups // 2

    def products(first, last):
        size = (last - first) * piece
        for which in range(2):
            tile = k if which == 0 else 1 - k
            active = has_tiles if which == 0 else takes

            @pl.when(active)
            def _():
                if which == 1:
                    for j in range(first, last):
                        for h in range(chunks):
                            sib_copy(1 - k, j, h).wait_recv()
                part = split(tiles[tile, first * piece : last * piece, :])
                at = pl.ds(pl.multiple_of(tile * (groups * piece) + first * piece, size), size)
                update_ref[:, at] = dot3((q_hi[...], q_lo[...]), part, NT)

    for j in range(halfway // 2):
        chain(j)
    for o in range(1, planes):
        fold_arrival(o).wait_recv()
        fsib_copy(o, k).start()
    for o in range(1, groups):
        inv_arrival(o).wait_recv()
        isib_copy(o, k).start()
    for j in range(halfway // 2, halfway):
        chain(j)
    for o in range(1, groups):
        isib_copy(o, 1 - k).wait_recv()
    inverse = split(inv_t[...])
    g_hi[...], g_lo[...] = split(dot3(inverse, inverse, NT))
    for j in range(halfway, halfway + halfway // 2):
        chain(j)
    for j in range(groups):
        @pl.when((z != c) & (c != j))
        def _():
            for h in range(chunks):
                rb_arrival(j, h).wait_recv()
    for j in range(halfway + halfway // 2, groups):
        @pl.when((z == c))
        def _():
            chain(j)
    q_hi[...], q_lo[...] = split(dot3(split(tiles[slot]), (g_hi[...], g_lo[...]), NN))
    for o in range(planes):
        fsib_copy(o, 1 - k).wait_recv()
    corr_ref[...] = dot3((q_hi[...], q_lo[...]), split(fold[...]), NN)
    done = halfway + halfway // 2
    ready = (done // per) * per
    for first in range(0, ready, per):
        products(first, first + per)
    for j in range(done, groups):
        @pl.when(z > c)
        def _():
            chain(j)
    for first in range(ready, groups, per):
        products(first, min(first + per, groups))

    for h in range(chunks):
        for o in range(1, groups):
            rb_copy(o, h).wait_send()
    for o in range(1, planes):
        fold_copy(o).wait_send()
    for o in range(planes):
        fsib_copy(o, k).wait_send()
    for o in range(1, groups):
        inv_copy(o).wait_send()
        isib_copy(o, k).wait_send()

    @pl.when(relays)
    def _():
        for j in range(groups):
            for h in range(chunks):
                up_copy(j, h).wait_send()

    @pl.when(gives)
    def _():
        for j in range(groups):
            for h in range(chunks):
                sib_copy(k, j, h).wait_send()


def solution(mesh):
    rows_axis = mesh.shape["row"]
    groups = mesh.shape["col"]
    planes = rows_axis // 2
    chunks = 2

    def on_device(trailing, panel, inv_factor, later_series, fold_series, fold_len):
        rows_here, cols_here = trailing.shape
        piece, width = panel.shape
        series = fold_series.shape[1]
        assert rows_axis % 2 == 0 and cols_here == 2 * rows_here and groups <= planes
        dma = pltpu.SemaphoreType.DMA
        vmem = pl.BlockSpec(memory_space=pltpu.VMEM)
        update, corr = pl.pallas_call(
            functools.partial(kernel, planes, groups, chunks),
            out_shape=(
                jax.ShapeDtypeStruct((rows_here, cols_here), F32),
                jax.ShapeDtypeStruct((rows_here, series), F32),
            ),
            in_specs=[vmem] * 3,
            out_specs=(vmem, vmem),
            scratch_shapes=[
                pltpu.VMEM((3, rows_here, width), F32),
                pltpu.VMEM((width, width), F32),
                pltpu.VMEM((width, series), F32),
                pltpu.VMEM((rows_here, width), BF16),
                pltpu.VMEM((rows_here, width), BF16),
                pltpu.VMEM((width, width), BF16),
                pltpu.VMEM((width, width), BF16),
                dma((groups, chunks)), dma((groups, chunks)),
                dma((groups, chunks)), dma((groups, chunks)),
                dma((groups, chunks)), dma((groups, chunks)),
                dma((planes,)), dma((planes,)), dma((planes,)), dma((planes,)),
                dma((groups,)), dma((groups,)), dma((groups,)), dma((groups,)),
            ],
            compiler_params=pltpu.CompilerParams(
                collective_id=0, has_side_effects=True, vmem_limit_bytes=40 * 1024 * 1024
            ),
        )(panel, inv_factor, fold_series)
        row_pos = lax.axis_index("row")
        col_pos = lax.axis_index("col")
        col_tile = (col_pos * cols_here + jnp.arange(cols_here, dtype=jnp.int32)) // rows_here
        lower = col_tile <= row_pos
        new_trailing = jnp.where(lower[None, :], trailing - update, trailing)
        active = row_pos < fold_len
        new_series = jnp.where(active[None, :], later_series - corr, later_series)
        return (new_trailing, new_series)

    in_specs = (
        P("row", "col"),
        P(("row", "col"), None),
        P(None, "col"),
        P("row", "col"),
        P("row", "col"),
        P("col"),
    )
    out_specs = (P("row", "col"), P("row", "col"))
    return jax.shard_map(
        on_device, mesh=mesh, in_specs=in_specs, out_specs=out_specs, check_vma=False
    )
```

time: 127 us -> 59.9 us (0.47)
  the two profiles are of different devices: /device:TPU:0 before, /device:TPU:25 now
where the time goes in v1:
time: 59.9 us; the launch traced here: 59.6 us
  Pallas kernels  51 us (85%)
  other arithmetic  5.23 us (9%)
  local copies, waits for them, and re-layouts  2.74 us (5%)
  between operations  0.66 us (1%)
    pallas_call x1, Pallas kernels, on_device(): pl.pallas_call(functools.partial(kernel, planes, groups, chunks), out_sha...  51 us
    select_n x1, other arithmetic, on_device(): new_trailing = jnp.where(lower[None, :], trailing - update, trailing)  3.6 us
    unnamed x8, local copies, waits for them, and re-layouts  2.74 us

profile of v1, /device:TPU:25, one launch (start us, length us, event | category | flops | bytes accessed | tf_op | source)
XLA Modules:
  0.0 59.6 jit_solution(10346421473264933693)
XLA Ops:
  0.6 0.7 %broadcast_compare_fusion = pred[256]{0:T(512)(128)(4,1)S(1)} fusion(s32[256]{0:T(256)} %param.11, s32[]{:T(128)S(6)} %axis_index.25), kind=kLoop, calls=%fused_computation.12 | loop fusion | flops 256 | bytes 1284 | tf_op jit(solution)/shard_map/lt | solution.py:329
  1.3 0.0 copy-start
  1.3 0.9 %copy-done = f32[128,512]{1,0:T(8,128)S(1)} copy-done((f32[128,512]{1,0:T(8,128)S(1)}, f32[128,512]{1,0:T(8,128)}, u32[]{:S(2)}) %copy-start) | copy-done | bytes 262168
  2.3 0.0 copy-start.1
  2.3 0.9 %copy-done.1 = f32[512,128]{1,0:T(8,128)S(1)} copy-done((f32[512,128]{1,0:T(8,128)S(1)}, f32[512,128]{1,0:T(8,128)}, u32[]{:S(2)}) %copy-start.1) | copy-done | bytes 262168
  3.2 0.0 copy-start.2
  3.2 0.8 %copy-done.2 = f32[64,256]{1,0:T(8,128)S(1)} copy-done((f32[64,256]{1,0:T(8,128)S(1)}, f32[64,256]{1,0:T(8,128)}, u32[]{:S(2)}) %copy-start.2) | copy-done | bytes 65560
  4.1 51.0 %shard_map.77 = (f32[512,1024]{1,0:T(8,128)S(1)}, f32[512,256]{1,0:T(8,128)S(1)}) custom-call(f32[128,512]{1,0:T(8,128)S(1)} %copy-done, f32[512,128]{1,0:T(8,128)S(1)} %copy-done.1, f32[64,256]{1,0:T(8,128)S(1)} %copy-done.2), custom_call_target="tpu_custom_call" | custom-call | tf_op jit(solution)/shard_map/pallas_call | solution.py:298
  55.1 0.0 copy-start.3
  55.1 3.6 %subtract_select_fusion = f32[512,1024]{1,0:T(8,128)} fusion(f32[512,1024]{1,0:T(8,128)} %param.6, f32[512,1024]{1,0:T(8,128)S(1)} %get-tuple-element.4, pred[1024]{0:T(1024)(128)(4,1)S(1)} %fusion.1), kind=kLoop, calls=%fused_computation | loop fusion | flops 1048576 | bytes 6292480 | tf_op jit(solution)/shard_map/jit(_where)/select_n | solution.py:328
  58.7 0.0 copy-done.3
  58.7 0.9 %subtract_select_fusion.1 = f32[512,256]{1,0:T(8,128)} fusion(f32[512,256]{1,0:T(8,128)S(1)} %copy-done.3, f32[512,256]{1,0:T(8,128)S(1)} %get-tuple-element.5, pred[256]{0:T(512)(128)(4,1)S(1)} %broadcast_compare_fusion), kind=kLoop, calls=%fused_computation.1 | loop fusion | flops 262144 | bytes 1573120 | tf_op jit(solution)/shard_map/jit(_where)/select_n | solution.py:330
  (1 shorter events, 0.0 us)
Async XLA Ops:
  1.3 1.0 %copy-start = (f32[128,512]{1,0:T(8,128)S(1)}, f32[128,512]{1,0:T(8,128)}, u32[]{:S(2)}) copy-start(f32[128,512]{1,0:T(8,128)} %panel_ref.1) | copy-start | bytes 786436
  2.3 0.9 %copy-start.1 = (f32[512,128]{1,0:T(8,128)S(1)}, f32[512,128]{1,0:T(8,128)}, u32[]{:S(2)}) copy-start(f32[512,128]{1,0:T(8,128)} %inv_ref.1) | copy-start | bytes 786436
  3.2 0.8 %copy-start.2 = (f32[64,256]{1,0:T(8,128)S(1)}, f32[64,256]{1,0:T(8,128)}, u32[]{:S(2)}) copy-start(f32[64,256]{1,0:T(8,128)} %fold_ref.1) | copy-start | bytes 196612
  55.1 3.6 %copy-start.3 = (f32[512,256]{1,0:T(8,128)S(1)}, f32[512,256]{1,0:T(8,128)}, u32[]{:S(2)}) copy-start(f32[512,256]{1,0:T(8,128)} %param.9) | copy-start | bytes 1572868

commit v2 on v1

--- a/solution.py
+++ b/solution.py
@@ -26,9 +26,9 @@
 
 def kernel(
     planes, groups, chunks,
-    panel_ref, inv_ref, fold_ref,
-    update_ref, corr_ref,
-    tiles, inv_t, fold, q_hi, q_lo, g_hi, g_lo,
+    trailing_ref, panel_ref, inv_ref, later_ref, fold_ref, len_ref,
+    out_ref, series_ref,
+    tiles, inv_in, inv_t, fold, lens, q_hi, q_lo, g_hi, g_lo, local,
     rb_send, rb_recv, up_send, up_recv, sib_send, sib_recv,
     fold_send, fold_recv, fsib_send, fsib_recv,
     inv_send, inv_recv, isib_send, isib_recv,
@@ -166,10 +166,19 @@
     takes = (z > c) | ((z == c) & (k == 1))
 
     own = pl.ds(pl.multiple_of(c * piece, piece), piece)
-    tiles[slot, own, :] = panel_ref[...]
-    fold[pl.ds(pl.multiple_of(row * fold_rows, fold_rows), fold_rows), :] = fold_ref[...]
-    inv_t[pl.ds(pl.multiple_of(c * inv_cols, inv_cols), inv_cols), :] = inv_ref[...].T
-
+    fetches = [
+        pltpu.make_async_copy(src, dst, local.at[n])
+        for n, (src, dst) in enumerate((
+            (panel_ref, tiles.at[slot, own]),
+            (fold_ref, fold_at(z, k)),
+            (inv_ref, inv_in),
+            (trailing_ref, out_ref),
+            (later_ref, series_ref),
+            (len_ref, lens),
+        ))
+    ]
+    for fetch in fetches:
+        fetch.start()
     pl.semaphore_wait(barrier, planes + groups - 1)
 
     def chain(j):
@@ -190,14 +199,44 @@
             def _():
                 sib_copy(k, j, h).start()
 
-    for h in range(chunks):
-        for o in range(1, groups):
-            rb_copy(o, h).start()
+    ordered = (z < groups) & (z != c) & (z + 1 < planes)
+
+    def is_first(o):
+        return ordered & ((c + o) % groups == z)
+
+    fetches[0].wait()
+    for o in range(1, groups):
+        @pl.when(is_first(o))
+        def _():
+            for h in range(chunks):
+                rb_copy(o, h).start()
+
+    fetches[1].wait()
     fsib_copy(0, k).start()
     for o in range(1, planes):
         fold_copy(o).start()
-    for o in range(1, groups):
-        inv_copy(o).start()
+    fetches[2].wait()
+    inv_t[pl.ds(pl.multiple_of(c * inv_cols, inv_cols), inv_cols), :] = inv_in[...].T
+
+    def send_rest():
+        for o in range(1, groups):
+            @pl.when(is_first(o))
+            def _():
+                for h in range(chunks):
+                    rb_copy(o, h).wait_send()
+        for o in range(1, groups):
+            @pl.when(jnp.logical_not(is_first(o)))
+            def _():
+                for h in range(chunks):
+                    rb_copy(o, h).start()
+        for o in range(1, groups):
+            inv_copy(o).start()
+
+    early = (z <= c) | (z + 1 >= planes)
+
+    @pl.when(early)
+    def _():
+        send_rest()
 
     per = max(1, min(groups, 256 // piece))
     halfway = groups // 2
@@ -216,10 +255,15 @@
                             sib_copy(1 - k, j, h).wait_recv()
                 part = split(tiles[tile, first * piece : last * piece, :])
                 at = pl.ds(pl.multiple_of(tile * (groups * piece) + first * piece, size), size)
-                update_ref[:, at] = dot3((q_hi[...], q_lo[...]), part, NT)
+                out_ref[:, at] = out_ref[:, at] - dot3((q_hi[...], q_lo[...]), part, NT)
 
     for j in range(halfway // 2):
         chain(j)
+
+    @pl.when(jnp.logical_not(early))
+    def _():
+        send_rest()
+
     for o in range(1, planes):
         fold_arrival(o).wait_recv()
         fsib_copy(o, k).start()
@@ -246,7 +290,11 @@
     q_hi[...], q_lo[...] = split(dot3(split(tiles[slot]), (g_hi[...], g_lo[...]), NN))
     for o in range(planes):
         fsib_copy(o, 1 - k).wait_recv()
-    corr_ref[...] = dot3((q_hi[...], q_lo[...]), split(fold[...]), NN)
+    correction = dot3((q_hi[...], q_lo[...]), split(fold[...]), NN)
+    for fetch in fetches[3:]:
+        fetch.wait()
+    later = series_ref[...]
+    series_ref[...] = jnp.where(row < lens[...], later - correction, later)
     done = halfway + halfway // 2
     ready = (done // per) * per
     for first in range(0, ready, per):
@@ -258,9 +306,11 @@
     for first in range(ready, groups, per):
         products(first, min(first + per, groups))
 
-    for h in range(chunks):
-        for o in range(1, groups):
-            rb_copy(o, h).wait_send()
+    for o in range(1, groups):
+        @pl.when(jnp.logical_not(is_first(o)))
+        def _():
+            for h in range(chunks):
+                rb_copy(o, h).wait_send()
     for o in range(1, planes):
         fold_copy(o).wait_send()
     for o in range(planes):
@@ -286,7 +336,7 @@
     rows_axis = mesh.shape["row"]
     groups = mesh.shape["col"]
     planes = rows_axis // 2
-    chunks = 2
+    chunks = 4
 
     def on_device(trailing, panel, inv_factor, later_series, fold_series, fold_len):
         rows_here, cols_here = trailing.shape
@@ -295,22 +345,25 @@
         assert rows_axis % 2 == 0 and cols_here == 2 * rows_here and groups <= planes
         dma = pltpu.SemaphoreType.DMA
         vmem = pl.BlockSpec(memory_space=pltpu.VMEM)
-        update, corr = pl.pallas_call(
+        return pl.pallas_call(
             functools.partial(kernel, planes, groups, chunks),
             out_shape=(
                 jax.ShapeDtypeStruct((rows_here, cols_here), F32),
                 jax.ShapeDtypeStruct((rows_here, series), F32),
             ),
-            in_specs=[vmem] * 3,
+            in_specs=[pl.BlockSpec(memory_space=pltpu.HBM)] * 6,
             out_specs=(vmem, vmem),
             scratch_shapes=[
                 pltpu.VMEM((3, rows_here, width), F32),
+                pltpu.VMEM(inv_factor.shape, F32),
                 pltpu.VMEM((width, width), F32),
                 pltpu.VMEM((width, series), F32),
+                pltpu.VMEM((1, series), jnp.int32),
                 pltpu.VMEM((rows_here, width), BF16),
                 pltpu.VMEM((rows_here, width), BF16),
                 pltpu.VMEM((width, width), BF16),
                 pltpu.VMEM((width, width), BF16),
+                dma((6,)),
                 dma((groups, chunks)), dma((groups, chunks)),
                 dma((groups, chunks)), dma((groups, chunks)),
                 dma((groups, chunks)), dma((groups, chunks)),
@@ -318,17 +371,9 @@
                 dma((groups,)), dma((groups,)), dma((groups,)), dma((groups,)),
             ],
             compiler_params=pltpu.CompilerParams(
-                collective_id=0, has_side_effects=True, vmem_limit_bytes=40 * 1024 * 1024
+                collective_id=0, has_side_effects=True, vmem_limit_bytes=32 * 1024 * 1024
             ),
-        )(panel, inv_factor, fold_series)
-        row_pos = lax.axis_index("row")
-        col_pos = lax.axis_index("col")
-        col_tile = (col_pos * cols_here + jnp.arange(cols_here, dtype=jnp.int32)) // rows_here
-        lower = col_tile <= row_pos
-        new_trailing = jnp.where(lower[None, :], trailing - update, trailing)
-        active = row_pos < fold_len
-        new_series = jnp.where(active[None, :], later_series - corr, later_series)
-        return (new_trailing, new_series)
+        )(trailing, panel, inv_factor, later_series, fold_series, fold_len.reshape(1, series))
 
     in_specs = (
         P("row", "col"),

time: 59.9 us -> 65.3 us (1.090)
  local copies, waits for them, and re-layouts: 2.74 us -> 8.16 us
  other arithmetic: 5.23 us -> 0 us
  Pallas kernels: 51 us -> 56.2 us
    unnamed x8 -> x14, local copies, waits for them, and re-layouts: 2.74 us -> 8.16 us
    pallas_call x1, Pallas kernels: 51 us -> 56.2 us  [on_device(): pl.pallas_call(functools.partial(kernel, planes, groups, chunks), out_sha...]
    select_n x2 -> x0, other arithmetic: 4.52 us -> none  [the longest x1 3.6 us: on_device(): new_trailing = jnp.where(lower[None, :], trailing - update, trailing)]
    lt x1 -> x0, other arithmetic: 0.69 us -> none  [on_device(): active = row_pos < fold_len]
where the time goes in v2:
time: 65.3 us; the launch traced here: 65 us
  Pallas kernels  56.2 us (86%)
  local copies, waits for them, and re-layouts  8.16 us (12%)
    pallas_call x1, Pallas kernels, on_device(): pl.pallas_call(functools.partial(kernel, planes, groups, chunks), out_sha...  56.2 us
    unnamed x14, local copies, waits for them, and re-layouts  8.16 us

profile of v2, /device:TPU:25, one launch (start us, length us, event | category | flops | bytes accessed | tf_op | source)
XLA Modules:
  0.0 65.0 jit_solution(16964605625515252047)
XLA Ops:
  0.6 0.0 copy-start
  0.6 1.6 %copy-done = f32[512,1024]{1,0:T(8,128)S(1)} copy-done((f32[512,1024]{1,0:T(8,128)S(1)}, f32[512,1024]{1,0:T(8,128)}, u32[]{:S(2)}) %copy-start) | copy-done | bytes 2097176
  2.2 0.0 copy-start.1
  2.2 1.0 %copy-done.1 = f32[512,256]{1,0:T(8,128)S(1)} copy-done((f32[512,256]{1,0:T(8,128)S(1)}, f32[512,256]{1,0:T(8,128)}, u32[]{:S(2)}) %copy-start.1) | copy-done | bytes 524312
  3.3 0.0 copy-start.2
  3.3 0.9 %copy-done.2 = f32[128,512]{1,0:T(8,128)S(1)} copy-done((f32[128,512]{1,0:T(8,128)S(1)}, f32[128,512]{1,0:T(8,128)}, u32[]{:S(2)}) %copy-start.2) | copy-done | bytes 262168
  4.2 0.0 copy-start.3
  4.2 0.9 %copy-done.3 = f32[512,128]{1,0:T(8,128)S(1)} copy-done((f32[512,128]{1,0:T(8,128)S(1)}, f32[512,128]{1,0:T(8,128)}, u32[]{:S(2)}) %copy-start.3) | copy-done | bytes 262168
  5.2 0.0 copy-start.4
  5.2 0.8 %copy-done.4 = f32[64,256]{1,0:T(8,128)S(1)} copy-done((f32[64,256]{1,0:T(8,128)S(1)}, f32[64,256]{1,0:T(8,128)}, u32[]{:S(2)}) %copy-start.4) | copy-done | bytes 65560
  6.0 0.0 copy-start.5
  6.0 0.7 %copy-done.5 = s32[256]{0:T(256)S(1)} copy-done((s32[256]{0:T(256)S(1)}, s32[256]{0:T(256)}, u32[]{:S(2)}) %copy-start.5) | copy-done | bytes 1048
  6.7 56.2 %shard_map.77 = (f32[512,1024]{1,0:T(8,128)S(1)}, f32[512,256]{1,0:T(8,128)S(1)}) custom-call(f32[512,1024]{1,0:T(8,128)S(1)} %copy-done, f32[128,512]{1,0:T(8,128)S(1)} %copy-done.2, f32[512,128]{1,0:T(8,128)S(1)} %copy-done.3, f32[512,256]{1,0:T(8,128)S(1)} %copy-done.1, f32[64,256]{1,0:T(8,128)S(1)} %copy-done.4, s32[1,256]{1,0:T(1,128)S(1)} %bitcast.1), custom_call_target="tpu_custom_call" | custom-call | tf_op jit(solution)/shard_map/pallas_call | solution.py:348
  62.9 1.3 %copy.10 = f32[512,1024]{1,0:T(8,128)} copy(f32[512,1024]{1,0:T(8,128)S(1)} %get-tuple-element.4) | data formatting | bytes 4194304
  64.2 0.8 %copy.11 = f32[512,256]{1,0:T(8,128)} copy(f32[512,256]{1,0:T(8,128)S(1)} %get-tuple-element.5) | data formatting | bytes 1048576
Async XLA Ops:
  0.6 1.6 %copy-start = (f32[512,1024]{1,0:T(8,128)S(1)}, f32[512,1024]{1,0:T(8,128)}, u32[]{:S(2)}) copy-start(f32[512,1024]{1,0:T(8,128)} %trailing_ref.1) | copy-start | bytes 6291460
  2.2 1.0 %copy-start.1 = (f32[512,256]{1,0:T(8,128)S(1)}, f32[512,256]{1,0:T(8,128)}, u32[]{:S(2)}) copy-start(f32[512,256]{1,0:T(8,128)} %later_ref.1) | copy-start | bytes 1572868
  3.3 0.9 %copy-start.2 = (f32[128,512]{1,0:T(8,128)S(1)}, f32[128,512]{1,0:T(8,128)}, u32[]{:S(2)}) copy-start(f32[128,512]{1,0:T(8,128)} %panel_ref.1) | copy-start | bytes 786436
  4.2 0.9 %copy-start.3 = (f32[512,128]{1,0:T(8,128)S(1)}, f32[512,128]{1,0:T(8,128)}, u32[]{:S(2)}) copy-start(f32[512,128]{1,0:T(8,128)} %inv_ref.1) | copy-start | bytes 786436
  5.2 0.8 %copy-start.4 = (f32[64,256]{1,0:T(8,128)S(1)}, f32[64,256]{1,0:T(8,128)}, u32[]{:S(2)}) copy-start(f32[64,256]{1,0:T(8,128)} %fold_ref.1) | copy-start | bytes 196612
  6.0 0.7 %copy-start.5 = (s32[256]{0:T(256)S(1)}, s32[256]{0:T(256)}, u32[]{:S(2)}) copy-start(s32[256]{0:T(256)} %param.11) | copy-start | bytes 3076

commit v3 on v2

--- a/solution.py
+++ b/solution.py
@@ -218,25 +218,40 @@
     fetches[2].wait()
     inv_t[pl.ds(pl.multiple_of(c * inv_cols, inv_cols), inv_cols), :] = inv_in[...].T
 
-    def send_rest():
+    for h in range(chunks):
+        for o in range(1, groups):
+            @pl.when(jnp.logical_not(is_first(o)))
+            def _():
+                rb_copy(o, h).start()
+    for o in range(1, groups):
+        @pl.when(jnp.logical_not(is_first(o)))
+        def _():
+            inv_copy(o).start()
+
+    def send_last():
         for o in range(1, groups):
             @pl.when(is_first(o))
             def _():
                 for h in range(chunks):
                     rb_copy(o, h).wait_send()
-        for o in range(1, groups):
-            @pl.when(jnp.logical_not(is_first(o)))
-            def _():
-                for h in range(chunks):
-                    rb_copy(o, h).start()
-        for o in range(1, groups):
-            inv_copy(o).start()
-
-    early = (z <= c) | (z + 1 >= planes)
-
-    @pl.when(early)
-    def _():
-        send_rest()
+                inv_copy(o).start()
+
+    below = z > c
+
+    def relay(first, last):
+        @pl.when(below)
+        def _():
+            for j in range(first, last):
+                chain(j)
+
+    @pl.when(z == c)
+    def _():
+        for j in range(groups):
+            chain(j)
+
+    @pl.when(jnp.logical_not(below))
+    def _():
+        send_last()
 
     per = max(1, min(groups, 256 // piece))
     halfway = groups // 2
@@ -257,36 +272,29 @@
                 at = pl.ds(pl.multiple_of(tile * (groups * piece) + first * piece, size), size)
                 out_ref[:, at] = out_ref[:, at] - dot3((q_hi[...], q_lo[...]), part, NT)
 
-    for j in range(halfway // 2):
-        chain(j)
-
-    @pl.when(jnp.logical_not(early))
-    def _():
-        send_rest()
+    relay(0, halfway // 2)
+
+    @pl.when(below)
+    def _():
+        send_last()
 
     for o in range(1, planes):
         fold_arrival(o).wait_recv()
         fsib_copy(o, k).start()
+    relay(halfway // 2, halfway)
     for o in range(1, groups):
         inv_arrival(o).wait_recv()
         isib_copy(o, k).start()
-    for j in range(halfway // 2, halfway):
-        chain(j)
     for o in range(1, groups):
         isib_copy(o, 1 - k).wait_recv()
     inverse = split(inv_t[...])
     g_hi[...], g_lo[...] = split(dot3(inverse, inverse, NT))
-    for j in range(halfway, halfway + halfway // 2):
-        chain(j)
+    relay(halfway, halfway + halfway // 2)
     for j in range(groups):
         @pl.when((z != c) & (c != j))
         def _():
             for h in range(chunks):
                 rb_arrival(j, h).wait_recv()
-    for j in range(halfway + halfway // 2, groups):
-        @pl.when((z == c))
-        def _():
-            chain(j)
     q_hi[...], q_lo[...] = split(dot3(split(tiles[slot]), (g_hi[...], g_lo[...]), NN))
     for o in range(planes):
         fsib_copy(o, 1 - k).wait_recv()
@@ -299,10 +307,7 @@
     ready = (done // per) * per
     for first in range(0, ready, per):
         products(first, first + per)
-    for j in range(done, groups):
-        @pl.when(z > c)
-        def _():
-            chain(j)
+    relay(done, groups)
     for first in range(ready, groups, per):
         products(first, min(first + per, groups))
 
@@ -371,7 +376,7 @@
                 dma((groups,)), dma((groups,)), dma((groups,)), dma((groups,)),
             ],
             compiler_params=pltpu.CompilerParams(
-                collective_id=0, has_side_effects=True, vmem_limit_bytes=32 * 1024 * 1024
+                collective_id=0, has_side_effects=True, vmem_limit_bytes=56 * 1024 * 1024
             ),
         )(trailing, panel, inv_factor, later_series, fold_series, fold_len.reshape(1, series))
 

time: 65.3 us -> 50.5 us (0.77)
  Pallas kernels: 56.2 us -> 45.6 us
  local copies, waits for them, and re-layouts: 8.16 us -> 4.01 us
    pallas_call x1, Pallas kernels: 56.2 us -> 45.6 us  [on_device(): pl.pallas_call(functools.partial(kernel, planes, groups, chunks), out_sha...]
    unnamed x14 -> x4, local copies, waits for them, and re-layouts: 8.16 us -> 4.01 us
where the time goes in v3:
time: 50.5 us; the launch traced here: 50.3 us
  Pallas kernels  45.6 us (90%)
  local copies, waits for them, and re-layouts  4.01 us (8%)
  between operations  0.65 us (1%)
    pallas_call x1, Pallas kernels, on_device(): pl.pallas_call(functools.partial(kernel, planes, groups, chunks), out_sha...  45.6 us
    unnamed x4, local copies, waits for them, and re-layouts  4.01 us

profile of v3, /device:TPU:25, one launch (start us, length us, event | category | flops | bytes accessed | tf_op | source)
XLA Modules:
  0.0 50.3 jit_solution(4862786319151686656)
XLA Ops:
  0.6 45.6 %shard_map.77 = (f32[512,1024]{1,0:T(8,128)}, f32[512,256]{1,0:T(8,128)}) custom-call(f32[512,1024]{1,0:T(8,128)} %trailing_ref.1, f32[128,512]{1,0:T(8,128)} %panel_ref.1, f32[512,128]{1,0:T(8,128)} %inv_ref.1, f32[512,256]{1,0:T(8,128)} %later_ref.1, f32[64,256]{1,0:T(8,128)} %fold_ref.1, s32[1,256]{1,0:T(1,128)} %bitcast.1), custom_call_target="tpu_custom_call" | custom-call | tf_op jit(solution)/shard_map/pallas_call | solution.py:353
  46.3 0.0 copy-start
  46.3 3.2 %copy.10 = f32[512,1024]{1,0:T(8,128)} copy(f32[512,1024]{1,0:T(8,128)} %get-tuple-element.4) | data formatting | bytes 4194304
  49.5 0.0 copy-done
  49.5 0.8 %copy.11 = f32[512,256]{1,0:T(8,128)} copy(f32[512,256]{1,0:T(8,128)S(1)} %copy-done) | data formatting | bytes 1048576
Async XLA Ops:
  46.3 3.2 %copy-start = (f32[512,256]{1,0:T(8,128)S(1)}, f32[512,256]{1,0:T(8,128)}, u32[]{:S(2)}) copy-start(f32[512,256]{1,0:T(8,128)} %get-tuple-element.5) | copy-start | bytes 1572868

commit v4 on v3

--- a/solution.py
+++ b/solution.py
@@ -238,8 +238,10 @@
 
     below = z > c
 
-    def relay(first, last):
-        @pl.when(below)
+    top = below & (z + 1 >= planes)
+
+    def relay(first, last, where=below):
+        @pl.when(where)
         def _():
             for j in range(first, last):
                 chain(j)
@@ -282,6 +284,7 @@
         fold_arrival(o).wait_recv()
         fsib_copy(o, k).start()
     relay(halfway // 2, halfway)
+    relay(halfway, groups, below & relays)
     for o in range(1, groups):
         inv_arrival(o).wait_recv()
         isib_copy(o, k).start()
@@ -289,7 +292,7 @@
         isib_copy(o, 1 - k).wait_recv()
     inverse = split(inv_t[...])
     g_hi[...], g_lo[...] = split(dot3(inverse, inverse, NT))
-    relay(halfway, halfway + halfway // 2)
+    relay(halfway, halfway + halfway // 2, top)
     for j in range(groups):
         @pl.when((z != c) & (c != j))
         def _():
@@ -307,7 +310,7 @@
     ready = (done // per) * per
     for first in range(0, ready, per):
         products(first, first + per)
-    relay(done, groups)
+    relay(done, groups, top)
     for first in range(ready, groups, per):
         products(first, min(first + per, groups))
 

time: 50.5 us -> 49.8 us (0.986)
  the two profiles are of different devices: /device:TPU:25 before, /device:TPU:17 now
where the time goes in v4:
time: 49.8 us; the launch traced here: 49.6 us
  Pallas kernels  45 us (90%)
  local copies, waits for them, and re-layouts  4.01 us (8%)
  between operations  0.65 us (1%)
    pallas_call x1, Pallas kernels, on_device(): pl.pallas_call(functools.partial(kernel, planes, groups, chunks), out_sha...  45 us
    unnamed x4, local copies, waits for them, and re-layouts  4.01 us

profile of v4, /device:TPU:17, one launch (start us, length us, event | category | flops | bytes accessed | tf_op | source)
XLA Modules:
  0.0 49.6 jit_solution(6829166054833111146)
XLA Ops:
  0.6 45.0 %shard_map.77 = (f32[512,1024]{1,0:T(8,128)}, f32[512,256]{1,0:T(8,128)}) custom-call(f32[512,1024]{1,0:T(8,128)} %trailing_ref.1, f32[128,512]{1,0:T(8,128)} %panel_ref.1, f32[512,128]{1,0:T(8,128)} %inv_ref.1, f32[512,256]{1,0:T(8,128)} %later_ref.1, f32[64,256]{1,0:T(8,128)} %fold_ref.1, s32[1,256]{1,0:T(1,128)} %bitcast.1), custom_call_target="tpu_custom_call" | custom-call | tf_op jit(solution)/shard_map/pallas_call | solution.py:356
  45.6 0.0 copy-start
  45.6 3.2 %copy.10 = f32[512,1024]{1,0:T(8,128)} copy(f32[512,1024]{1,0:T(8,128)} %get-tuple-element.4) | data formatting | bytes 4194304
  48.8 0.0 copy-done
  48.8 0.8 %copy.11 = f32[512,256]{1,0:T(8,128)} copy(f32[512,256]{1,0:T(8,128)S(1)} %copy-done) | data formatting | bytes 1048576
Async XLA Ops:
  45.6 3.2 %copy-start = (f32[512,256]{1,0:T(8,128)S(1)}, f32[512,256]{1,0:T(8,128)}, u32[]{:S(2)}) copy-start(f32[512,256]{1,0:T(8,128)} %get-tuple-element.5) | copy-start | bytes 1572868

commit v5 on v4

--- a/solution.py
+++ b/solution.py
@@ -284,7 +284,7 @@
         fold_arrival(o).wait_recv()
         fsib_copy(o, k).start()
     relay(halfway // 2, halfway)
-    relay(halfway, groups, below & relays)
+    relay(halfway, halfway + halfway // 2, below & relays)
     for o in range(1, groups):
         inv_arrival(o).wait_recv()
         isib_copy(o, k).start()
@@ -292,6 +292,7 @@
         isib_copy(o, 1 - k).wait_recv()
     inverse = split(inv_t[...])
     g_hi[...], g_lo[...] = split(dot3(inverse, inverse, NT))
+    relay(halfway + halfway // 2, groups, below & relays)
     relay(halfway, halfway + halfway // 2, top)
     for j in range(groups):
         @pl.when((z != c) & (c != j))

time: 49.8 us -> 48.8 us (0.980)
  the two profiles are of different devices: /device:TPU:17 before, /device:TPU:25 now
where the time goes in v5:
time: 48.8 us; the launch traced here: 48.6 us
  Pallas kernels  43.9 us (90%)
  local copies, waits for them, and re-layouts  4.01 us (8%)
  between operations  0.65 us (1%)
    pallas_call x1, Pallas kernels, on_device(): pl.pallas_call(functools.partial(kernel, planes, groups, chunks), out_sha...  43.9 us
    unnamed x4, local copies, waits for them, and re-layouts  4.01 us

profile of v5, /device:TPU:25, one launch (start us, length us, event | category | flops | bytes accessed | tf_op | source)
XLA Modules:
  0.0 48.6 jit_solution(2316839990445332205)
XLA Ops:
  0.6 43.9 %shard_map.77 = (f32[512,1024]{1,0:T(8,128)}, f32[512,256]{1,0:T(8,128)}) custom-call(f32[512,1024]{1,0:T(8,128)} %trailing_ref.1, f32[128,512]{1,0:T(8,128)} %panel_ref.1, f32[512,128]{1,0:T(8,128)} %inv_ref.1, f32[512,256]{1,0:T(8,128)} %later_ref.1, f32[64,256]{1,0:T(8,128)} %fold_ref.1, s32[1,256]{1,0:T(1,128)} %bitcast.1), custom_call_target="tpu_custom_call" | custom-call | tf_op jit(solution)/shard_map/pallas_call | solution.py:357
  44.6 0.0 copy-start
  44.6 3.2 %copy.10 = f32[512,1024]{1,0:T(8,128)} copy(f32[512,1024]{1,0:T(8,128)} %get-tuple-element.4) | data formatting | bytes 4194304
  47.8 0.0 copy-done
  47.8 0.8 %copy.11 = f32[512,256]{1,0:T(8,128)} copy(f32[512,256]{1,0:T(8,128)S(1)} %copy-done) | data formatting | bytes 1048576
Async XLA Ops:
  44.6 3.2 %copy-start = (f32[512,256]{1,0:T(8,128)S(1)}, f32[512,256]{1,0:T(8,128)}, u32[]{:S(2)}) copy-start(f32[512,256]{1,0:T(8,128)} %get-tuple-element.5) | copy-start | bytes 1572868
